TPU v7x, 256 devices: a whole 4x4x8 slice. The times are simulated.
256 devices in a mesh: fsdp: 16 (over x_lo, z), factor: 16 (over x_hi, y, core).
Axes of the slice: x: 4 (x_hi: 2, x_lo: 2; x = x_hi * 2 + x_lo), y: 4, z: 8, core: 2. Of those that a mesh axis runs over, the one named last changes fastest.
Arguments:
- activations: bfloat16 [256, 16, 16, 512], P(('fsdp', 'factor')), may hold values from -12 to 12
- cotangent: bfloat16 [256, 16, 16, 512], P(('fsdp', 'factor')), may hold values from -0.23632812 to 0.23632812
- weight: bfloat16 [4608, 512], P('fsdp'), may hold values from -0.09375 to 0.09375
- a_factor_old: float32 [4608, 4608], P('factor', 'fsdp'), may hold values from -0.11785113 to 5, as said below
- g_factor_old: float32 [512, 512], P('factor'), may hold values from -0.35355339 to 5, as said below
- a_inverse: float32 [4608, 4608], P('fsdp', 'factor'), may hold values from -0.09375 to 0.09375
- g_inverse: float32 [512, 512], replicated, may hold values from -0.25 to 0.25
Outputs:
- conv_out: bfloat16 [256, 16, 16, 512], P(('fsdp', 'factor'))
- a_factor: float32 [4608, 4608], P('factor', 'fsdp')
- g_factor: float32 [512, 512], P('factor')
- natural_grad: bfloat16 [4608, 512], P('fsdp', 'factor')
Inputs may be any that keep to these rules, and one draw needn't show every extreme that they name: `a_factor_old`: a symmetric matrix. `g_factor_old`: a symmetric matrix.
All inputs are finite; a program needn't handle non-finite values.
Results may differ from a plain program's by a relative error of at most 0.0017.
Values may be sent and summed in bfloat16 or wider, within the bound.
A program may use at most 192 MiB of HBM per device.

v0:
```python
import jax
import jax.numpy as jnp
from jax import lax
from jax.sharding import PartitionSpec as P


def unfold(images):
    side = images.shape[1]
    padded = jnp.pad(images, ((0, 0), (1, 1), (1, 1), (0, 0)))
    tap_list = [
        padded[:, row_off : row_off + side, col_off : col_off + side, :]
        for row_off in range(3)
        for col_off in range(3)
    ]
    return jnp.concatenate(tap_list, axis=3).reshape(-1, 9 * images.shape[3])


def contract(first_op, second_op):
    return lax.dot_general(
        first_op, second_op, (((0,), (0,)), ((), ())), preferred_element_type=jnp.float32
    )


def per_device(activations, cotangent, weight, a_factor_old, g_factor_old, a_inverse, g_inverse):
    channels = activations.shape[3]
    own_patches = unfold(activations)
    own_cot = cotangent.reshape(-1, channels)
    factor_index = lax.axis_index("factor")
    rows_per = a_factor_old.shape[0]
    row_start = factor_index * rows_per
    conv_total = jnp.dot(
        own_patches,
        lax.all_gather(weight, "fsdp", axis=0, tiled=True),
        preferred_element_type=jnp.float32,
    )
    conv_out = conv_total.astype(jnp.bfloat16).reshape(activations.shape)
    patches = unfold(lax.all_gather(activations, "factor", axis=0, tiled=True))
    a_partial = contract(lax.dynamic_slice_in_dim(patches, row_start, rows_per, 1), patches)
    grad_partial = lax.psum_scatter(
        contract(own_patches, own_cot), "factor", scatter_dimension=0, tiled=True
    )
    a_summed = lax.psum_scatter(a_partial, "fsdp", scatter_dimension=1, tiled=True)
    pixel_total = float(
        activations.shape[1]
        * activations.shape[2]
        * lax.axis_size("fsdp")
        * lax.axis_size("factor")
    )
    a_factor = 0.5 * a_factor_old + 0.5 * (a_summed / pixel_total)
    grad_rows = lax.psum(grad_partial, "fsdp")
    g_partial = contract(own_cot, own_cot)
    g_rows_count = g_factor_old.shape[0]
    g_summed = lax.psum(g_partial, ("fsdp", "factor"))
    g_rows = lax.dynamic_slice_in_dim(g_summed, factor_index * g_rows_count, g_rows_count, 0)
    g_factor = 0.5 * g_factor_old + 0.5 * g_rows
    mixed = jnp.dot(
        grad_rows, g_inverse, precision=lax.Precision.HIGHEST, preferred_element_type=jnp.float32
    )
    partial_rows = jnp.dot(
        a_inverse, mixed, precision=lax.Precision.HIGHEST, preferred_element_type=jnp.float32
    )
    summed_rows = lax.psum(partial_rows, "factor")
    tile_width = channels // lax.axis_size("factor")
    result_tile = lax.dynamic_slice_in_dim(summed_rows, factor_index * tile_width, tile_width, 1)
    return (conv_out, a_factor, g_factor, result_tile.astype(jnp.bfloat16))


def solution(mesh):
    return jax.shard_map(
        per_device,
        mesh=mesh,
        in_specs=(
            P(("fsdp", "factor"), None, None, None),
            P(("fsdp", "factor"), None, None, None),
            P("fsdp", None),
            P("factor", "fsdp"),
            P("factor", None),
            P("fsdp", "factor"),
            P(),
        ),
        out_specs=(
            P(("fsdp", "factor"), None, None, None),
            P("factor", "fsdp"),
            P("factor", None),
            P("fsdp", "factor"),
        ),
        check_vma=False,
    )
```

profile of v0, /device:TPU:0, one launch (start us, length us, event | category | flops | bytes accessed | tf_op | source)
XLA Modules:
  0.0 599.1 jit_solution(16298183459508021695)
XLA Ops:
  8.0 0.0 copy-start
  8.0 0.0 all-gather.5.cloned.1.call-start
  8.1 0.7 all-gather.5.cloned.1.call-update
  8.8 0.0 reduce-scatter.5.cloned.1.call-start
  8.8 1.0 fusion.10
  9.8 1.0 fusion.11
  10.8 1.0 fusion.12
  11.8 1.0 fusion.13
  12.8 1.0 constant_dynamic-update-slice_fusion
  13.8 1.0 fusion.14
  14.8 1.0 fusion.15
  15.9 1.0 fusion.16
  16.8 0.1 fusion.17
  16.9 1.4 copy-done.6
  18.3 5.1 convolution_bitcast_fusion
  23.4 0.0 reduce-scatter.5.cloned.1.call-update
  23.4 0.0 all-reduce.6.cloned.1.call-start
  23.4 1.3 convolution_bitcast_fusion.2
  24.8 0.0 all-reduce.6.cloned.1.call-update
  24.8 0.0 all-gather.3.cloned.1.call-start
  24.8 0.7 all-gather.3.cloned.1.call-update
  25.5 0.2 all-reduce.8.cloned.1.call-start
  25.8 47.5 %all-gather.5.cloned.1.call-done = bf16[16,16,16,512]{3,2,1,0:T(8,128)(2,1)} async-done(((bf16[1,16,16,512]{3,2,1,0:T(8,128)(2,1)}), bf16[16,16,16,512]{3,2,1,0:T(8,128)(2,1)}) %all-gather.5.cloned.1.call-update) | async-done | bytes 4194320 | tf_op jit(solution)/shard_map/all_gather | solution.py:37
  73.3 5.6 fusion
  78.9 2.7 fusion.1
  81.6 4.1 fusion.2
  85.6 4.2 fusion.3
  89.9 2.8 constant_dynamic-update-slice_fusion.1
  92.6 4.2 fusion.4
  96.9 4.1 fusion.5
  100.9 2.7 fusion.6
  103.7 4.2 fusion.7
  107.9 82.9 %reduce-scatter.5.cloned.1.call-done = f32[288,512]{1,0:T(8,128)} async-done(((f32[4608,512]{1,0:T(8,128)}), f32[288,512]{1,0:T(8,128)}) %reduce-scatter.5.cloned.1.call-update) | async-done | bytes 589840 | tf_op jit(solution)/shard_map/reduce_scatter | solution.py:39
  190.8 0.0 all-reduce.8.cloned.1.call-update
  190.9 0.0 reduce-scatter.7.cloned.1.call-start
  190.9 27.4 %convolution_bitcast_fusion.1 = f32[4608,288]{1,0:T(8,128)} fusion(bf16[4096,4608]{1,0:T(8,128)(2,1)} %bitcast.27, s32[]{:T(128)S(6)} %select_n.7), kind=kOutput, calls=%fused_computation.9 | convolution fusion | flops 10871635968 | bytes 46202884
  218.3 0.0 reduce-scatter.7.cloned.1.call-update
  218.4 91.2 %all-reduce.6.cloned.1.call-done = f32[512,512]{1,0:T(8,128)} async-done(((f32[512,512]{1,0:T(8,128)}), f32[512,512]{1,0:T(8,128)}) %all-reduce.6.cloned.1.call-update) | async-done | bytes 1048592 | tf_op jit(solution)/shard_map/psum | solution.py:53
  309.5 1.5 add_multiply_fusion
  311.0 5.2 convolution_convert_fusion
  316.2 130.5 %all-reduce.8.cloned.1.call-done = f32[288,512]{1,0:T(8,128)} async-done(((f32[288,512]{1,0:T(8,128)}), f32[288,512]{1,0:T(8,128)}) %all-reduce.8.cloned.1.call-update) | async-done | bytes 589840 | tf_op jit(solution)/shard_map/psum | solution.py:50
  446.8 2.2 fusion.21
  449.0 1.1 convolution_bitcast_fusion.3
  450.1 138.8 %all-reduce.9 = bf16[288,512]{1,0:T(8,128)(2,1)S(1)} all-reduce(f32[288,512]{1,0:T(8,128)S(1)} %convolution_bitcast_fusion.3), channel_id=1, replica_groups=mesh['fsdp'=16,'factor'=16] {'factor'}, use_global_device_ids=true, to_apply=%region_4.5 | all-reduce | flops 147456 | bytes 884736 | tf_op jit(solution)/shard_map/psum | solution.py:62
  589.0 0.1 dynamic-slice_convert_fusion
  589.1 0.7 copy.12
  589.8 1.2 copy.14
  591.0 0.8 multiply_add_fusion
  (16 shorter events, 0.0 us)
Async XLA Ops:
  8.0 438.8 %copy-start = (f32[512,512]{1,0:T(8,128)S(1)}, f32[512,512]{1,0:T(8,128)}, u32[]{:S(2)}) copy-start(f32[512,512]{1,0:T(8,128)} %param.13) | copy-start | bytes 3145732
  8.0 8.8 %copy-start.2 = (bf16[1,16,16,512]{3,2,1,0:T(8,128)(2,1)S(1)}, bf16[1,16,16,512]{3,2,1,0:T(8,128)(2,1)}, u32[]{:S(2)}) copy-start(bf16[1,16,16,512]{3,2,1,0:T(8,128)(2,1)} %param.7) | copy-start | bytes 786436
  8.0 10.3 %copy-start.7 = (bf16[1,16,16,512]{3,2,1,0:T(8,128)(2,1)S(1)}, bf16[1,16,16,512]{3,2,1,0:T(8,128)(2,1)}, u32[]{:S(2)}) copy-start(bf16[1,16,16,512]{3,2,1,0:T(8,128)(2,1)} %param.8) | copy-start | bytes 786436
  8.0 65.3 %all-gather.5.cloned.1.call-start = ((), (), s32[]{:S(2)}) async-start(), calls=%async_computation.3 | async-start | bytes 4456448 | tf_op jit(solution)/shard_map/all_gather | solution.py:37
  8.8 182.1 %reduce-scatter.5.cloned.1.call-start = ((), (), s32[]{:S(2)}) async-start(), calls=%async_computation.5 | async-start | bytes 10027008 | tf_op jit(solution)/shard_map/reduce_scatter | solution.py:39
  16.9 1.4 copy-start.6
  23.4 286.2 %all-reduce.6.cloned.1.call-start = ((), (), s32[]{:S(2)}) async-start(), calls=%async_computation.4 | async-start | bytes 2097152 | tf_op jit(solution)/shard_map/psum | solution.py:53
  24.8 286.2 %all-gather.3.cloned.1.call-start = ((), (), s32[]{:S(2)}) async-start(), calls=%async_computation.2 | async-start | bytes 5013504 | tf_op jit(solution)/shard_map/all_gather | solution.py:33
  25.5 421.2 %all-reduce.8.cloned.1.call-start = ((), (), s32[]{:S(2)}) async-start(), calls=%async_computation.6 | async-start | bytes 1179648 | tf_op jit(solution)/shard_map/psum | solution.py:50
  73.3 5.6 copy-start.1
  190.9 398.9 %reduce-scatter.7.cloned.1.call-start = ((), (), s32[]{:S(2)}) async-start(), calls=%async_computation.7 | async-start | bytes 7520256
  218.3 91.2 %copy-start.5 = (f32[32,512]{1,0:T(8,128)S(1)}, f32[32,512]{1,0:T(8,128)}, u32[]{:S(2)}) copy-start(f32[32,512]{1,0:T(8,128)} %param.11) | copy-start | bytes 196612
  311.0 137.9 %copy-start.3 = (f32[288,288]{1,0:T(8,128)S(1)}, f32[288,288]{1,0:T(8,128)}, u32[]{:S(2)}) copy-start(f32[288,288]{1,0:T(8,128)} %param.12) | copy-start | bytes 995332
  316.2 274.8 %copy-start.4 = (f32[288,288]{1,0:T(8,128)S(1)}, f32[288,288]{1,0:T(8,128)}, u32[]{:S(2)}) copy-start(f32[288,288]{1,0:T(8,128)} %param.10) | copy-start | bytes 995332
Sparse Core Ops, SparseCore 0:
  11.6 61.6 all-gather.4
  77.9 112.8 reduce-scatter.4
  192.8 76.6 all-gather.2
Sparse Core Ops, SparseCore 1:
  30.2 279.3 all-reduce.5
  312.0 134.6 all-reduce.7
  449.4 88.0 reduce-scatter.6
where the time goes:
time: 600 us; the launch traced here: 599 us
  waiting for transfers between devices  354 us (59%)
  blocking collectives  139 us (23%)
  local copies, waits for them, and re-layouts  46 us (8%)
  matrix products  42.4 us (7%)
  between operations  15.6 us (3%)
    psum x1, blocking collectives, per_device(): summed_rows = lax.psum(partial_rows, 'factor')  139 us
    psum x1, waiting for transfers between devices, per_device(): grad_rows = lax.psum(grad_partial, 'fsdp')  131 us
    psum x1, waiting for transfers between devices, per_device(): g_summed = lax.psum(g_partial, ('fsdp', 'factor'))  91.2 us
    reduce_scatter x1, waiting for transfers between devices, per_device(): lax.psum_scatter(contract(own_patches, own_cot), 'factor', scatter_dimens...  82.9 us
    all_gather x1, waiting for transfers between devices, per_device(): patches = unfold(lax.all_gather(activations, 'factor', axis=0, tiled=True))  47.5 us
    unnamed x34, local copies, waits for them, and re-layouts  41.7 us
    unnamed x1, matrix products  27.4 us
  transfers between devices with their start and end apart: 6, of which 4 were waited for; matrix products, arithmetic and copies ran while one was open for 15% of the time, Pallas kernels for 0%

commit v1 on v0

v1 whole, which is shorter than its diff:
```python
import jax
import jax.numpy as jnp
from jax import lax
from jax.experimental import pallas as pl
from jax.experimental.pallas import tpu as pltpu
from jax.sharding import PartitionSpec as P

MESH = pl.DeviceIdType.MESH
F32 = jnp.float32
BF16 = jnp.bfloat16
X_BLOCKS = ((0, 0), (1, 1), (2, 2), (0, 1), (0, 2), (1, 0), (2, 0))
Y_PAIRS = ((0, 0, 5), (1, 1, 5), (2, 2, 5), (0, 1, 7), (0, 2, 7))
BLOCKS = 29


def kernel(
    x_ref, dy_ref, w_ref, a_old_ref, g_old_ref, a_inv_ref, g_inv_ref,
    conv_ref, a_ref, g_ref, ng_ref,
    x_all, x_t, xa_t, xb, z_send, z_all, z_sh, w_all,
    m_part, m_recv, m_piece, m_rows, n_send, n_recv,
    a_send, a_recv, a_sum, tile, g_send, g_recv, g_sum, g2_recv, g_piece, g_fin,
    c_send, c_recv,
    in_sem, xs_sem, xr_sem, xf_sem, zs_sem, zr_sem, zf_sem, ws_sem, wr_sem,
    ms_sem, mr_sem, mgs_sem, mgr_sem, ns_sem, nr_sem, as_sem, ar_sem, ts_sem, tr_sem,
    gs_sem, gr_sem, g2s_sem, g2r_sem, g3s_sem, g3r_sem, cs_sem, cr_sem,
):
    i = lax.axis_index("fsdp")
    j = lax.axis_index("factor")
    xh, y, core = j // 8, (j // 2) % 4, j % 2
    a = 2 * xh + core
    b = y
    sibling = j + 1 - 2 * core

    def remote(src, dst, send, recv, dev_i, dev_j):
        return pltpu.make_async_remote_copy(
            src_ref=src, dst_ref=dst, send_sem=send, recv_sem=recv,
            device_id=(dev_i, dev_j), device_id_type=MESH,
        )

    def each(lo, hi, body):
        def step(k, carry):
            body(k)
            return carry
        lax.fori_loop(lo, hi, step, 0)

    entry = pltpu.get_barrier_semaphore()

    def greet(k):
        pl.semaphore_signal(entry, inc=1, device_id=((i + k) % 16, j), device_id_type=MESH)
        pl.semaphore_signal(entry, inc=1, device_id=(i, (j + k) % 16), device_id_type=MESH)

    each(1, 16, greet)
    pl.semaphore_wait(entry, 30)
    each(1, 16, lambda k: pl.semaphore_signal(
        in_sem, inc=1, device_id=(i, (j + k) % 16), device_id_type=MESH))

    def x_out(k):
        return remote(x_ref.at[0], x_all.at[pl.ds(1, 16), j], xs_sem.at[k], xr_sem.at[j],
                      i, (j + 2 * k) % 16)

    each(1, 8, lambda k: x_out(k).start())
    x_sib = remote(x_ref.at[0], x_all.at[pl.ds(1, 16), j], xs_sem.at[0], xr_sem.at[j], i, sibling)
    x_sib.start()

    def w_out(k):
        return remote(w_ref.at[:, pl.ds(pl.multiple_of(128 * y, 128), 128)],
                      w_all.at[pl.ds(pl.multiple_of(288 * i, 32), 288)],
                      ws_sem.at[k], wr_sem.at[i], (i + k) % 16, j)

    each(1, 16, lambda k: w_out(k).start())

    x_all[0] = jnp.zeros((16, 16, 512), BF16)
    x_all[17] = jnp.zeros((16, 16, 512), BF16)
    x_all[1:17, pl.ds(j, 1)] = x_ref[0][:, None]
    w_all[pl.ds(pl.multiple_of(288 * i, 32), 288), :] = w_ref[:, pl.ds(pl.multiple_of(128 * y, 128), 128)]

    cot = dy_ref[0].reshape(256, 512)
    g1 = g_inv_ref[...].astype(BF16)
    rest = g_inv_ref[...] - g1.astype(F32)
    g2 = rest.astype(BF16)
    g3 = (rest - g2.astype(F32)).astype(BF16)
    z = jnp.dot(cot, g3, preferred_element_type=F32)
    z = z + jnp.dot(cot, g2, preferred_element_type=F32)
    z = z + jnp.dot(cot, g1, preferred_element_type=F32)
    hi = z.astype(BF16)
    lo = (z - hi.astype(F32)).astype(BF16)
    for q in range(4):
        z_send[q, :, :, 0:128] = hi[:, 128 * q:128 * q + 128].reshape(16, 16, 128)
        z_send[q, :, :, 128:256] = lo[:, 128 * q:128 * q + 128].reshape(16, 16, 128)

    def z_out(k):
        to = (j + 2 * k) % 16
        return remote(z_send.at[(to // 2) % 4], z_all.at[:, j], zs_sem.at[k], zr_sem.at[j], i, to)

    each(1, 8, lambda k: z_out(k).start())
    z_sib = remote(z_send.at[y], z_all.at[:, j], zs_sem.at[0], zr_sem.at[j], i, sibling)
    z_sib.start()
    z_all[:, pl.ds(j, 1)] = z_send[y][:, None]

    g_send[...] = lax.dot_general(
        cot, cot, (((0,), (0,)), ((), ())), preferred_element_type=F32).astype(BF16)

    def g_out(k):
        to = (j + k) % 16
        return remote(g_send.at[pl.ds(pl.multiple_of(32 * to, 32), 32)], g_recv.at[j],
                      gs_sem.at[k], gr_sem.at[j], i, to)

    each(1, 16, lambda k: g_out(k).start())
    g_recv[pl.ds(j, 1)] = g_send[pl.ds(pl.multiple_of(32 * j, 32), 32)][None]

    def x_fwd(k):
        src = (j + 16 - 2 * k) % 16
        here = x_all.at[pl.ds(1, 16), src]
        return remote(here, here, xf_sem.at[k], xr_sem.at[src], i, sibling)

    def x_forward(k):
        x_fwd(k).wait_recv()
        x_fwd(k).start()

    def z_fwd(k):
        src = (j + 16 - 2 * k) % 16
        here = z_all.at[:, src]
        return remote(here, here, zf_sem.at[k], zr_sem.at[src], i, sibling)

    def z_forward(k):
        z_fwd(k).wait_recv()
        z_fwd(k).start()

    each(1, 8, x_forward)

    def x_other(k):
        src = (sibling + 2 * k) % 16
        here = x_all.at[pl.ds(1, 16), src]
        remote(here, here, xf_sem.at[0], xr_sem.at[src], i, sibling).wait_recv()

    each(0, 8, x_other)

    col = lax.broadcasted_iota(jnp.int32, (128, 256), 1) % 16
    row = lax.broadcasted_iota(jnp.int32, (256, 128), 0) % 16

    def plane(v):
        at = pl.ds(pl.multiple_of(256 * v, 256), 256)
        x_t[:, at] = x_all[v].reshape(256, 512).T
        mid = x_t[pl.ds(pl.multiple_of(128 * a, 128), 128), at]
        wide = mid.astype(F32)
        xa_t[0:128, at] = jnp.where(col == 0, 0.0, pltpu.roll(wide, 1, 1)).astype(BF16)
        xa_t[128:256, at] = mid
        xa_t[256:384, at] = jnp.where(col == 15, 0.0, pltpu.roll(wide, 255, 1)).astype(BF16)
        mid = x_all[v, :, :, pl.ds(pl.multiple_of(128 * b, 128), 128)].reshape(256, 128)
        wide = mid.astype(F32)
        xb[at, 0:128] = jnp.where(row == 0, 0.0, pltpu.roll(wide, 1, 0)).astype(BF16)
        xb[at, 128:256] = mid
        xb[at, 256:384] = jnp.where(row == 15, 0.0, pltpu.roll(wide, 255, 0)).astype(BF16)

    each(0, 18, plane)

    each(1, 8, z_forward)

    def z_other(k):
        src = (sibling + 2 * k) % 16
        here = z_all.at[:, src]
        remote(here, here, zf_sem.at[0], zr_sem.at[src], i, sibling).wait_recv()

    each(0, 8, z_other)

    row2 = lax.broadcasted_iota(jnp.int32, (256, 256), 0) % 16

    def z_plane(v):
        at = pl.ds(pl.multiple_of(256 * v, 256), 256)
        mid = z_all[v].reshape(256, 256)
        wide = mid.astype(F32)
        z_sh[0, at, :] = jnp.where(row2 == 15, 0.0, pltpu.roll(wide, 255, 0)).astype(BF16)
        z_sh[1, at, :] = mid
        z_sh[2, at, :] = jnp.where(row2 == 0, 0.0, pltpu.roll(wide, 1, 0)).astype(BF16)

    each(0, 16, z_plane)

    def m_chunk(k):
        r = 9 * a + k
        tap = r // 4
        lhs = x_t[pl.ds(pl.multiple_of(128 * (r % 4), 128), 128),
                  pl.ds(pl.multiple_of(256 * (tap // 3), 256), 4096)]
        both = jnp.dot(lhs, z_sh[tap % 3], preferred_element_type=F32)
        m_part[pl.ds(pl.multiple_of(128 * k, 128), 128), :] = both[:, 0:128] + both[:, 128:256]

    each(0, 9, m_chunk)

    def m_out(k):
        to = (i + k) % 16
        return remote(m_part.at[pl.ds(pl.multiple_of(72 * to, 8), 72)], m_recv.at[i],
                      ms_sem.at[k], mr_sem.at[i], to, j)

    each(1, 16, lambda k: m_out(k).start())
    m_recv[pl.ds(i, 1)] = m_part[pl.ds(pl.multiple_of(72 * i, 8), 72)][None]

    def a_out(to):
        return remote(a_send.at[pl.ds(pl.multiple_of(256 * to, 256), 256)], a_recv.at[i],
                      as_sem.at[to], ar_sem.at[i], to, j)

    def a_start(to):
        @pl.when(to != i)
        def _():
            a_out(to).start()

    at_block, sent = 0, 0
    for row_y, col_y, count in Y_PAIRS:
        part = jnp.dot(xa_t[:, 256 * row_y:256 * row_y + 4096],
                       xb[256 * col_y:256 * col_y + 4096, :], preferred_element_type=F32)
        for row_x, col_x in X_BLOCKS[:count]:
            a_send[128 * at_block:128 * at_block + 128, :] = part[
                128 * row_x:128 * row_x + 128, 128 * col_x:128 * col_x + 128].astype(BF16)
            at_block += 1
        if at_block == BLOCKS:
            a_send[128 * BLOCKS:128 * BLOCKS + 128, :] = jnp.zeros((128, 128), BF16)
            at_block += 1
        each(sent, at_block // 2, a_start)
        sent = at_block // 2

    @pl.when(i < 15)
    def _():
        a_recv[pl.ds(i, 1)] = a_send[pl.ds(pl.multiple_of(256 * i, 256), 256)][None]

    def w_in(k):
        src = (i + 16 - k) % 16
        here = w_all.at[pl.ds(pl.multiple_of(288 * src, 32), 288)]
        remote(here, here, ws_sem.at[k], wr_sem.at[src], src, j).wait_recv()

    each(1, 16, w_in)
    conv_row = lax.broadcasted_iota(jnp.int32, (256, 128), 0) % 16

    def conv_image(q):
        image = 8 * xh + 2 * q + core
        parts = []
        for dx in range(3):
            total = jnp.zeros((256, 128), F32)
            for dy in range(3):
                total = total + jnp.dot(
                    x_all[dy:dy + 16, pl.ds(image, 1)].reshape(256, 512),
                    w_all[512 * (3 * dy + dx):512 * (3 * dy + dx) + 512, :],
                    preferred_element_type=F32)
            parts.append(total)
        out = parts[1] + jnp.where(conv_row == 0, 0.0, pltpu.roll(parts[0], 1, 0))
        out = out + jnp.where(conv_row == 15, 0.0, pltpu.roll(parts[2], 255, 0))
        c_send[pl.ds(q, 1)] = out.astype(BF16)[None]

    each(0, 4, conv_image)
    here_y = pl.ds(pl.multiple_of(128 * y, 128), 128)

    def c_out(k):
        q = (y + k) % 4
        return remote(c_send.at[q], c_recv.at[:, here_y], cs_sem.at[k], cr_sem.at[y],
                      i, 8 * xh + 2 * q + core)

    each(1, 4, lambda k: c_out(k).start())
    c_recv[:, here_y] = c_send[y]

    def m_in(k):
        src = (i + 16 - k) % 16
        here = m_recv.at[src]
        remote(here, here, ms_sem.at[k], mr_sem.at[src], src, j).wait_recv()

    each(1, 16, m_in)
    total = m_recv[0]
    for k in range(1, 16):
        total = total + m_recv[k]
    m_piece[...] = total
    pl.semaphore_wait(in_sem, 15)
    m_to = 4 * a + i // 4

    def m_spot(rho, chunk):
        return m_rows.at[pl.ds(pl.multiple_of(72 * rho, 8), 72),
                         pl.ds(pl.multiple_of(128 * chunk, 128), 128)]

    def mg_out(to):
        return remote(m_piece, m_spot(i % 4, b), mgs_sem.at[to], mgr_sem.at[4 * (i % 4) + b], to, m_to)

    def mg_self():
        return pltpu.make_async_copy(m_piece, m_spot(i % 4, b), mgr_sem.at[4 * (i % 4) + b])

    def mg_start(k):
        to = (i + k) % 16
        mine = (to == i) & (m_to == j)

        @pl.when(jnp.logical_not(mine))
        def _():
            mg_out(to).start()

        @pl.when(mine)
        def _():
            mg_self().start()

    each(0, 16, mg_start)

    def g_in(k):
        src = (j + 16 - k) % 16
        here = g_recv.at[src]
        remote(here, here, gs_sem.at[k], gr_sem.at[src], i, src).wait_recv()

    each(1, 16, g_in)
    total = g_recv[0].astype(F32)
    for k in range(1, 16):
        total = total + g_recv[k].astype(F32)
    g_sum[...] = total

    def g_spot(ref, who):
        return ref.at[pl.ds(pl.multiple_of(8 * (who // 4), 8), 8),
                      pl.ds(pl.multiple_of(128 * (who % 4), 128), 128)]

    def g2_out(k):
        to = (i + k) % 16
        return remote(g_spot(g_sum, to), g2_recv.at[i], g2s_sem.at[k], g2r_sem.at[i], to, j)

    each(1, 16, lambda k: g2_out(k).start())
    g2_recv[pl.ds(i, 1)] = g_sum[pl.ds(pl.multiple_of(8 * (i // 4), 8), 8),
                                 pl.ds(pl.multiple_of(128 * (i % 4), 128), 128)][None]

    @pl.when(i < 15)
    def _():
        def a_in(k):
            src = (i + 16 - k) % 16
            here = a_recv.at[src]
            remote(here, here, as_sem.at[0], ar_sem.at[src], src, j).wait_recv()

        each(1, 16, a_in)
        for half in range(2):
            span = slice(128 * half, 128 * half + 128)
            total = a_recv[0, span].astype(F32)
            for k in range(1, 16):
                total = total + a_recv[k, span].astype(F32)
            a_sum[2 * half] = total
            a_sum[2 * half + 1] = total.T

    def spread(act):
        def one(n):
            half = n // 32
            turned = (n // 16) % 2
            yp, xp, tj, ti = (n // 8) % 2, (n // 4) % 2, (n // 2) % 2, n % 2
            k = 2 * i + half
            flat = k < 15
            ey = jnp.where(flat, 0, jnp.where(k < 22, 1, 2))
            s = jnp.where(flat, k % 5, (k + 6) % 7)
            ex = jnp.where(s < 3, 0, jnp.where(s < 5, s - 2, 4 - s))
            row_y = jnp.where(flat, k // 5, yp)
            row_x = jnp.where(s < 3, s, jnp.where(s < 5, 0, s - 4)) + xp
            ok = (k < BLOCKS) & ((yp == 0) | (ey == 1)) & ((xp == 0) | (ex == 1) | (ex == -1))
            ok = ok & ((turned == 0) | (ey != 0) | (ex != 0))
            first = 4 * (3 * row_y + row_x) + a
            second = 4 * (3 * (row_y + ey) + row_x + ex) + b
            r = jnp.where(turned == 0, first, second)
            c = jnp.where(turned == 0, second, first)
            to_j = (4 * r) // 9 + tj
            to_i = (4 * c) // 9 + ti
            ok = ok & (to_j <= (128 * r + 127) // 288) & (to_i <= (128 * c + 127) // 288)
            at_r = r - (9 * to_j) // 4
            at_c = c - (9 * to_i) // 4
            src = a_sum.at[2 * half + turned]
            dst = tile.at[pl.ds(pl.multiple_of(128 * at_r, 128), 128),
                          pl.ds(pl.multiple_of(128 * at_c, 128), 128)]
            mine = (to_i == i) & (to_j == j)
            arrived = tr_sem.at[3 * at_r + at_c]

            @pl.when(ok & jnp.logical_not(mine))
            def _():
                act(remote(src, dst, ts_sem.at[n], arrived, to_i, to_j))

            if act is start:
                @pl.when(ok & mine)
                def _():
                    pltpu.make_async_copy(src, dst, arrived).start()

        each(0, 64, one)

    def start(copy):
        copy.start()

    def sent_off(copy):
        copy.wait_send()

    spread(start)

    for q in range(4):
        for chunk in range(4):
            here = m_spot(q, chunk)
            remote(here, here, mgs_sem.at[0], mgr_sem.at[4 * q + chunk], i, sibling).wait_recv()
    prod = jnp.dot(a_inv_ref[...], m_rows[...], precision=lax.Precision.HIGHEST,
                   preferred_element_type=F32)
    lane = lax.broadcasted_iota(jnp.int32, (72, 128), 1) // 32
    for to in range(16):
        piece = jnp.zeros((72, 128), F32)
        for q in range(4):
            block = prod[72 * q:72 * q + 72, 128 * (to // 4):128 * (to // 4) + 128]
            shift = (32 * (q - to % 4)) % 128
            if shift:
                block = pltpu.roll(block, shift, 1)
            piece = jnp.where(lane == q, block, piece)
        n_send[to] = piece

    def n_out(k):
        to = (j + k) % 16
        return remote(n_send.at[to], n_recv.at[j], ns_sem.at[k], nr_sem.at[j], i, to)

    each(1, 16, lambda k: n_out(k).start())
    n_recv[pl.ds(j, 1)] = n_send[pl.ds(j, 1)]

    def g2_in(k):
        src = (i + 16 - k) % 16
        here = g2_recv.at[src]
        remote(here, here, g2s_sem.at[k], g2r_sem.at[src], src, j).wait_recv()

    each(1, 16, g2_in)
    total = g2_recv[0]
    for k in range(1, 16):
        total = total + g2_recv[k]
    g_piece[...] = total

    def g3_out(k):
        return remote(g_piece, g_spot(g_fin, i), g3s_sem.at[k], g3r_sem.at[i], (i + k) % 16, j)

    each(1, 16, lambda k: g3_out(k).start())
    g_fin[pl.ds(pl.multiple_of(8 * (i // 4), 8), 8),
          pl.ds(pl.multiple_of(128 * (i % 4), 128), 128)] = total

    def c_in(k):
        q = (y + 4 - k) % 4
        here = c_recv.at[:, pl.ds(pl.multiple_of(128 * q, 128), 128)]
        remote(here, here, cs_sem.at[k], cr_sem.at[q], i, sibling).wait_recv()

    each(1, 4, c_in)
    conv_ref[...] = c_recv[...]

    for q in range(9):
        here = tile.at[pl.ds(128 * (q // 3), 128), pl.ds(128 * (q % 3), 128)]
        remote(here, here, ts_sem.at[0], tr_sem.at[q], i, sibling).wait_recv()
    rows = tile[pl.ds(pl.multiple_of(32 * (j % 4), 32), 288), :]
    rows = pltpu.roll(rows, (384 - 32 * (i % 4)) % 384, 1)[:, 0:288]
    a_ref[...] = 0.5 * a_old_ref[...] + (0.5 / 65536.0) * rows

    def g3_in(k):
        src = (i + 16 - k) % 16
        here = g_spot(g_fin, src)
        remote(here, here, g3s_sem.at[k], g3r_sem.at[src], src, j).wait_recv()

    each(1, 16, g3_in)
    g_ref[...] = 0.5 * g_old_ref[...] + 0.5 * g_fin[...]

    def n_in(k):
        src = (j + 16 - k) % 16
        here = n_recv.at[src]
        remote(here, here, ns_sem.at[k], nr_sem.at[src], i, src).wait_recv()

    each(1, 16, n_in)
    total = n_recv[0]
    for k in range(1, 16):
        total = total + n_recv[k]
    ng_ref[...] = total

    x_sib.wait_send()
    z_sib.wait_send()
    each(1, 8, lambda k: x_out(k).wait_send())
    each(1, 8, lambda k: z_out(k).wait_send())
    each(1, 8, lambda k: x_fwd(k).wait_send())
    each(1, 8, lambda k: z_fwd(k).wait_send())
    each(1, 4, lambda k: c_out(k).wait_send())

    def rest_sent(k):
        w_out(k).wait_send()
        g_out(k).wait_send()
        m_out(k).wait_send()
        g2_out(k).wait_send()
        g3_out(k).wait_send()
        n_out(k).wait_send()

    each(1, 16, rest_sent)

    def a_sent(to):
        @pl.when(to != i)
        def _():
            a_out(to).wait_send()

    each(0, 15, a_sent)

    def mg_sent(to):
        @pl.when(jnp.logical_not((to == i) & (m_to == j)))
        def _():
            mg_out(to).wait_send()

    each(0, 16, mg_sent)
    spread(sent_off)


def per_device(activations, cotangent, weight, a_factor_old, g_factor_old, a_inverse, g_inverse):
    vmem = pl.BlockSpec(memory_space=pltpu.VMEM)
    dma = pltpu.SemaphoreType.DMA
    conv, a_factor, g_factor, packed = pl.pallas_call(
        kernel,
        name="kfac_step",
        out_shape=(
            jax.ShapeDtypeStruct((256, 512), BF16),
            jax.ShapeDtypeStruct((288, 288), F32),
            jax.ShapeDtypeStruct((32, 512), F32),
            jax.ShapeDtypeStruct((72, 128), F32),
        ),
        in_specs=[vmem] * 7,
        out_specs=(vmem,) * 4,
        scratch_shapes=[
            pltpu.VMEM((18, 16, 16, 512), BF16),
            pltpu.VMEM((512, 4608), BF16),
            pltpu.VMEM((384, 4608), BF16),
            pltpu.VMEM((4608, 384), BF16),
            pltpu.VMEM((4, 16, 16, 256), BF16),
            pltpu.VMEM((16, 16, 16, 256), BF16),
            pltpu.VMEM((3, 4096, 256), BF16),
            pltpu.VMEM((4608, 128), BF16),
            pltpu.VMEM((1152, 128), F32),
            pltpu.VMEM((16, 72, 128), F32),
            pltpu.VMEM((72, 128), F32),
            pltpu.VMEM((288, 512), F32),
            pltpu.VMEM((16, 72, 128), F32),
            pltpu.VMEM((16, 72, 128), F32),
            pltpu.VMEM((3840, 128), BF16),
            pltpu.VMEM((16, 256, 128), BF16),
            pltpu.VMEM((4, 128, 128), F32),
            pltpu.VMEM((384, 384), F32),
            pltpu.VMEM((512, 512), BF16),
            pltpu.VMEM((16, 32, 512), BF16),
            pltpu.VMEM((32, 512), F32),
            pltpu.VMEM((16, 8, 128), F32),
            pltpu.VMEM((8, 128), F32),
            pltpu.VMEM((32, 512), F32),
            pltpu.VMEM((4, 256, 128), BF16),
            pltpu.VMEM((256, 512), BF16),
            pltpu.SemaphoreType.REGULAR,
            dma((8,)), dma((16,)), dma((8,)),
            dma((8,)), dma((16,)), dma((8,)),
            dma((16,)), dma((16,)),
            dma((16,)), dma((16,)), dma((16,)), dma((16,)),
            dma((16,)), dma((16,)),
            dma((16,)), dma((16,)), dma((64,)), dma((9,)),
            dma((16,)), dma((16,)), dma((16,)), dma((16,)), dma((16,)), dma((16,)),
            dma((4,)), dma((4,)),
        ],
        compiler_params=pltpu.CompilerParams(
            collective_id=0, has_side_effects=True, vmem_limit_bytes=56 * 1024 * 1024),
        cost_estimate=pl.CostEstimate(flops=15_000_000_000, bytes_accessed=4_000_000, transcendentals=0),
    )(activations, cotangent, weight, a_factor_old, g_factor_old, a_inverse, g_inverse)
    natural = packed.reshape(72, 4, 32).transpose(1, 0, 2).reshape(288, 32).astype(BF16)
    return conv.reshape(1, 16, 16, 512), a_factor, g_factor, natural


def solution(mesh):
    return jax.shard_map(
        per_device,
        mesh=mesh,
        in_specs=(
            P(("fsdp", "factor"), None, None, None),
            P(("fsdp", "factor"), None, None, None),
            P("fsdp", None),
            P("factor", "fsdp"),
            P("factor", None),
            P("fsdp", "factor"),
            P(),
        ),
        out_specs=(
            P(("fsdp", "factor"), None, None, None),
            P("factor", "fsdp"),
            P("factor", None),
            P("fsdp", "factor"),
        ),
        check_vma=False,
    )
```

time: 600 us -> 166 us (0.28)
  the two profiles are of different devices: /device:TPU:0 before, /device:TPU:184 now
where the time goes in v1:
time: 166 us
  Pallas kernels  161 us (97%)
  local copies, waits for them, and re-layouts  4.01 us (2%)
    pallas_call x1, Pallas kernels, per_device(): pl.pallas_call(kernel, name='kfac_step', out_shape=(jax.ShapeDtypeStruct(...  161 us

profile of v1, /device:TPU:184, one launch (start us, length us, event | category | flops | bytes accessed | tf_op | source)
XLA Modules:
  0.0 166.1 jit_solution(8233113497357440244)
XLA Ops:
  0.6 160.6 %kfac_step.1 = (bf16[256,512]{1,0:T(8,128)(2,1)}, f32[288,288]{1,0:T(8,128)}, f32[32,512]{1,0:T(8,128)}, f32[72,128]{1,0:T(8,128)}) custom-call(bf16[1,16,16,512]{3,2,1,0:T(8,128)(2,1)} %x_ref.1, bf16[1,16,16,512]{3,2,1,0:T(8,128)(2,1)} %dy_ref.1, bf16[288,512]{1,0:T(8,128)(2,1)} %w_ref.1, f32[288,288]{1,0:T(8,128)} %a_old_ref.1, f32[32,512]{1,0:T(8,128)} %g_old_ref.1, ...), custom_call_target="tpu_custom_call" | custom-call | flops 15000000512 | bytes 4000000 | tf_op jit(solution)/shard_map/kfac_step/pallas_call | solution.py:494
  161.2 0.0 copy-start
  161.2 0.8 convert_element_type.12
  162.0 0.1 copy.13
  162.2 0.7 convert_element_type.15
  162.9 1.7 %copy.18 = bf16[1,16,16,512]{3,2,1,0:T(8,128)(2,1)} copy(bf16[1,16,16,512]{3,2,1,0:T(8,128)(2,1)} %bitcast.6) | data formatting | bytes 524288
  164.6 0.0 copy-done
  164.6 0.0 copy-start.1
  164.6 0.8 copy.19
  165.3 0.1 copy-done.1
  165.4 0.6 copy.20
  (1 shorter events, 0.0 us)
Async XLA Ops:
  161.2 3.4 %copy-start = (f32[288,288]{1,0:T(8,128)S(1)}, f32[288,288]{1,0:T(8,128)}, u32[]{:S(2)}) copy-start(f32[288,288]{1,0:T(8,128)} %get-tuple-element.17) | copy-start | bytes 995332
  164.6 0.9 copy-start.1

commit v2 on v1

v2 whole, which is shorter than its diff:
```python
import jax
import jax.numpy as jnp
from jax import lax
from jax.experimental import pallas as pl
from jax.experimental.pallas import tpu as pltpu
from jax.sharding import PartitionSpec as P

MESH = pl.DeviceIdType.MESH
F32 = jnp.float32
BF16 = jnp.bfloat16
X_BLOCKS = ((0, 0), (1, 1), (2, 2), (0, 1), (0, 2), (1, 0), (2, 0))
COUNTS = (5, 5, 5, 7, 7)
BLOCKS = 29


def kernel(
    x_ref, dy_ref, w_ref, a_old_ref, g_old_ref, a_inv_ref, g_inv_ref,
    conv_ref, a_ref, g_ref, ng_ref,
    x_all, x_t, xa_t, xb, z_all, z_sh, w_all, a_acc, inv_both,
    m_part, m_recv, m_cols, m_piece, m_rows, n_send, n_recv,
    a_send, a_recv, a_sum, tile, g_send, g_recv, g_sum, g2_recv, g_piece, g_fin,
    c_send, c_recv,
    in_sem, inv_sem, xs_sem, xr_sem, xh_sem, xf_sem, zs_sem, zr_sem, zf_sem, ws_sem, wr_sem, wf_sem,
    ms_sem, mr_sem, mxs_sem, mxr_sem, mgs_sem, mgr_sem, ns_sem, nr_sem, as_sem, ar_sem, ts_sem, tr_sem,
    gs_sem, gr_sem, g2s_sem, g2r_sem, g3s_sem, g3r_sem, cs_sem, cr_sem,
):
    i = lax.axis_index("fsdp")
    j = lax.axis_index("factor")
    xh, y, core = j // 8, (j // 2) % 4, j % 2
    a = 2 * xh + core
    b = y
    sibling = j + 1 - 2 * core
    xl, z = i // 8, i % 8

    def remote(src, dst, send, recv, dev_i, dev_j):
        return pltpu.make_async_remote_copy(
            src_ref=src, dst_ref=dst, send_sem=send, recv_sem=recv,
            device_id=(dev_i, dev_j), device_id_type=MESH,
        )

    def each(lo, hi, body):
        def step(k, carry):
            body(k)
            return carry
        lax.fori_loop(lo, hi, step, 0)

    entry = pltpu.get_barrier_semaphore()

    def greet(k):
        pl.semaphore_signal(entry, inc=1, device_id=((i + k) % 16, j), device_id_type=MESH)
        pl.semaphore_signal(entry, inc=1, device_id=(i, (j + k) % 16), device_id_type=MESH)

    each(1, 16, greet)
    pl.semaphore_wait(entry, 30)
    each(1, 16, lambda k: pl.semaphore_signal(
        in_sem, inc=1, device_id=(i, (j + k) % 16), device_id_type=MESH))

    def image(half, step):
        return 8 * ((xh + half) % 2) + 2 * ((y + step + 4) % 4) + core

    def x_at(who, lo=0, size=256):
        return x_all.at[who, pl.ds(16 + lo, size)]

    def x_own(n):
        to = (image(0, 1), image(0, -1), image(1, 0), sibling)[n]
        return remote(x_ref, x_at(j), xs_sem.at[n], xr_sem.at[j], i, to)

    def x_pass(n):
        who = image(1, 0)
        return remote(x_at(who), x_at(who), xs_sem.at[4 + n], xr_sem.at[who], i, image(0, 1 - 2 * n))

    def x_half(half, n):
        step = 1 - 2 * n
        who = image(half, -step)
        here = x_at(who, 128 * n, 128)
        return remote(here, here, xs_sem.at[6 + 2 * half + n], (xr_sem, xh_sem)[n].at[who], i, image(0, step))

    def x_fwd(who):
        return remote(x_at(who), x_at(who), xf_sem.at[who], xr_sem.at[who], i, sibling)

    def x_got(who, lo=0, size=256, sem=None):
        here = x_at(who, lo, size)
        remote(here, here, xf_sem.at[who], (xr_sem if sem is None else sem).at[who], i, sibling).wait_recv()

    for n in range(4):
        x_own(n).start()

    def z_out(k):
        to = (j + 2 * k) % 16
        return remote(dy_ref.at[:, pl.ds(pl.multiple_of(128 * ((to // 2) % 4), 128), 128)],
                      z_all.at[j], zs_sem.at[k], zr_sem.at[j], i, to)

    each(1, 8, lambda k: z_out(k).start())
    here_y = pl.ds(pl.multiple_of(128 * y, 128), 128)
    z_sib = remote(dy_ref.at[:, here_y], z_all.at[j], zs_sem.at[0], zr_sem.at[j], i, sibling)
    z_sib.start()

    def w_at(who):
        return w_all.at[pl.ds(pl.multiple_of(288 * who, 32), 288)]

    def w_out(k):
        return remote(w_ref.at[:, here_y], w_at(i), ws_sem.at[k], wr_sem.at[i], (i + k) % 16, j)

    w_lo = 2 - core

    def w_each(body):
        def step(n, carry):
            body(2 * n + w_lo)
            return carry
        lax.fori_loop(0, 7 + core, step, 0)

    w_each(lambda k: w_out(k).start())

    inv_out = remote(a_inv_ref, inv_both.at[xl], inv_sem.at[0], inv_sem.at[1], (i + 8) % 16, j)
    inv_out.start()

    def clear(who):
        x_all[pl.ds(who, 1), 0:16] = jnp.zeros((1, 16, 512), BF16)
        x_all[pl.ds(who, 1), 272:288] = jnp.zeros((1, 16, 512), BF16)

    each(0, 16, clear)
    x_all[pl.ds(j, 1), 16:272] = x_ref[...][None]
    z_all[pl.ds(j, 1)] = dy_ref[:, here_y][None]
    w_all[pl.ds(pl.multiple_of(288 * i, 32), 288), :] = w_ref[:, here_y]
    inv_both[pl.ds(xl, 1)] = a_inv_ref[...][None]
    xb[256:288, :] = jnp.zeros((32, 384), BF16)
    for dx in range(3):
        z_sh[dx, 0:16] = jnp.zeros((16, 128), BF16)
        z_sh[dx, 272:288] = jnp.zeros((16, 128), BF16)
    a_acc[...] = jnp.zeros((5, 384, 384), F32)
    m_part[...] = jnp.zeros((1152, 128), F32)

    col = lax.broadcasted_iota(jnp.int32, (128, 256), 1) % 16
    row = lax.broadcasted_iota(jnp.int32, (256, 128), 0) % 16
    map_row = lax.broadcasted_iota(jnp.int32, (256, 384), 0) // 16
    none = jnp.zeros((256, 384), BF16)

    def terms(who):
        x_t[...] = x_all[pl.ds(who, 1), 16:272].reshape(256, 512).T
        mid = x_t[pl.ds(pl.multiple_of(128 * a, 128), 128), :]
        wide = mid.astype(F32)
        xa_t[0:128] = jnp.where(col == 0, 0.0, pltpu.roll(wide, 1, 1)).astype(BF16)
        xa_t[128:256] = mid
        xa_t[256:384] = jnp.where(col == 15, 0.0, pltpu.roll(wide, 255, 1)).astype(BF16)
        mid = x_all[pl.ds(who, 1), 16:272, here_y].reshape(256, 128)
        wide = mid.astype(F32)
        xb[0:256, 0:128] = jnp.where(row == 0, 0.0, pltpu.roll(wide, 1, 0)).astype(BF16)
        xb[0:256, 128:256] = mid
        xb[0:256, 256:384] = jnp.where(row == 15, 0.0, pltpu.roll(wide, 255, 0)).astype(BF16)
        mid = z_all[pl.ds(who, 1)].reshape(256, 128)
        wide = mid.astype(F32)
        z_sh[0, 16:272] = jnp.where(row == 15, 0.0, pltpu.roll(wide, 255, 0)).astype(BF16)
        z_sh[1, 16:272] = mid
        z_sh[2, 16:272] = jnp.where(row == 0, 0.0, pltpu.roll(wide, 1, 0)).astype(BF16)
        lhs = xa_t[...]
        flat = xb[0:256, :]
        a_acc[0] += jnp.dot(lhs, jnp.where(map_row == 15, none, flat), preferred_element_type=F32)
        a_acc[1] += jnp.dot(lhs, flat, preferred_element_type=F32)
        a_acc[2] += jnp.dot(lhs, jnp.where(map_row == 0, none, flat), preferred_element_type=F32)
        a_acc[3] += jnp.dot(lhs, xb[16:272, :], preferred_element_type=F32)
        a_acc[4] += jnp.dot(lhs, xb[32:288, :], preferred_element_type=F32)
        for k in range(9):
            r = 9 * a + k
            tap = r // 4
            part = jnp.dot(x_t[pl.ds(pl.multiple_of(128 * (r % 4), 128), 128), :],
                           z_sh[tap % 3, pl.ds(pl.multiple_of(32 - 16 * (tap // 3), 16), 256), :],
                           preferred_element_type=F32)
            m_part[128 * k:128 * k + 128, :] += part

    def z_fwd(who):
        return remote(z_all.at[who], z_all.at[who], zf_sem.at[who // 2], zr_sem.at[who], i, sibling)

    def z_got(who):
        remote(z_all.at[who], z_all.at[who], zf_sem.at[0], zr_sem.at[who], i, sibling).wait_recv()

    def hand_on(who):
        x_fwd(who).start()
        z_got(who)
        z_fwd(who).start()

    def from_ring(half, n):
        x_got(image(half, 2 * n - 1))
        x_half(half, n).start()
        hand_on(image(half, 2 * n - 1))

    def from_far(half):
        who = image(half, 2)
        x_got(who, 0, 128)
        x_got(who, 128, 128, xh_sem)
        hand_on(who)

    def arrivals(n, carry):
        @pl.when(n == 1)
        def _():
            from_ring(0, 0)
            from_ring(0, 1)
            x_got(image(1, 0))
            x_pass(0).start()
            x_pass(1).start()
            hand_on(image(1, 0))

        @pl.when(n == 3)
        def _():
            from_far(0)

        @pl.when(n == 5)
        def _():
            from_ring(1, 0)
            from_ring(1, 1)

        @pl.when(n == 7)
        def _():
            from_far(1)

        half = jnp.where((n == 3) | (n > 4), 1, 0)
        step = jnp.where((n == 0) | (n == 3), 0, jnp.where((n == 1) | (n == 5), 3, jnp.where((n == 2) | (n == 6), 1, 2)))
        mine = image(half, step)

        def one(c, carry):
            who = jnp.where(c == 0, mine, mine + 1 - 2 * core)

            @pl.when(c == 1)
            def _():
                x_got(who)
                z_got(who)

            terms(who)
            return carry

        return lax.fori_loop(0, 2, one, carry)

    lax.fori_loop(0, 8, arrivals, 0)

    def w_in(k):
        src = (i + 16 - k) % 16
        remote(w_at(src), w_at(src), ws_sem.at[k], wr_sem.at[src], src, j).wait_recv()

    def w_fwd(k):
        src = (i + 16 - k) % 16
        return remote(w_at(src), w_at(src), wf_sem.at[k], wr_sem.at[src], i, sibling)

    def w_forward(k):
        w_in(k)
        w_fwd(k).start()

    w_each(w_forward)

    def m_out(k):
        to = (i + k) % 16
        return remote(m_part.at[pl.ds(pl.multiple_of(72 * to, 8), 72)], m_recv.at[i],
                      ms_sem.at[k], mr_sem.at[i], to, j)

    each(1, 16, lambda k: m_out(k).start())
    m_recv[pl.ds(i, 1)] = m_part[pl.ds(pl.multiple_of(72 * i, 8), 72)][None]

    cot = dy_ref[...]
    g_send[...] = lax.dot_general(
        cot, cot, (((0,), (0,)), ((), ())), preferred_element_type=F32).astype(BF16)

    def g_out(k):
        to = (j + k) % 16
        return remote(g_send.at[pl.ds(pl.multiple_of(32 * to, 32), 32)], g_recv.at[j],
                      gs_sem.at[k], gr_sem.at[j], i, to)

    each(1, 16, lambda k: g_out(k).start())
    g_recv[pl.ds(j, 1)] = g_send[pl.ds(pl.multiple_of(32 * j, 32), 32)][None]

    def a_out(to):
        return remote(a_send.at[pl.ds(pl.multiple_of(256 * to, 256), 256)], a_recv.at[i],
                      as_sem.at[to], ar_sem.at[i], to, j)

    def a_start(to):
        @pl.when(to != i)
        def _():
            a_out(to).start()

    at_block, sent = 0, 0
    for combo, count in enumerate(COUNTS):
        part = a_acc[combo]
        for row_x, col_x in X_BLOCKS[:count]:
            a_send[128 * at_block:128 * at_block + 128, :] = part[
                128 * row_x:128 * row_x + 128, 128 * col_x:128 * col_x + 128].astype(BF16)
            at_block += 1
        if at_block == BLOCKS:
            a_send[128 * BLOCKS:128 * BLOCKS + 128, :] = jnp.zeros((128, 128), BF16)
            at_block += 1
        each(sent, at_block // 2, a_start)
        sent = at_block // 2

    @pl.when(i < 15)
    def _():
        a_recv[pl.ds(i, 1)] = a_send[pl.ds(pl.multiple_of(256 * i, 256), 256)][None]

    def w_other(k):
        @pl.when(k % 2 != core)
        def _():
            w_in(k)

    each(1, 16, w_other)
    conv_row = lax.broadcasted_iota(jnp.int32, (256, 128), 0) % 16

    def conv_image(q):
        who = 8 * xh + 2 * q + core
        parts = []
        for dx in range(3):
            total = jnp.zeros((256, 128), F32)
            for dy in range(3):
                total = total + jnp.dot(
                    x_all[pl.ds(who, 1), 16 * dy:16 * dy + 256].reshape(256, 512),
                    w_all[512 * (3 * dy + dx):512 * (3 * dy + dx) + 512, :],
                    preferred_element_type=F32)
            parts.append(total)
        out = parts[1] + jnp.where(conv_row == 0, 0.0, pltpu.roll(parts[0], 1, 0))
        out = out + jnp.where(conv_row == 15, 0.0, pltpu.roll(parts[2], 255, 0))
        c_send[pl.ds(q, 1)] = out.astype(BF16)[None]

    each(0, 4, conv_image)

    def c_out(k):
        q = (y + k) % 4
        return remote(c_send.at[q], c_recv.at[:, here_y], cs_sem.at[k], cr_sem.at[y],
                      i, 8 * xh + 2 * q + core)

    each(1, 4, lambda k: c_out(k).start())
    c_recv[:, here_y] = c_send[y]

    def m_in(k):
        src = (i + 16 - k) % 16
        here = m_recv.at[src]
        remote(here, here, ms_sem.at[k], mr_sem.at[src], src, j).wait_recv()

    each(1, 16, m_in)
    total = m_recv[0]
    for k in range(1, 16):
        total = total + m_recv[k]
    m_cols[pl.ds(y, 1)] = total[None]

    def mx_out(k):
        return remote(m_cols.at[y], m_cols.at[y], mxs_sem.at[k], mxr_sem.at[y], i, image_of(k))

    def image_of(k):
        return 8 * xh + 2 * ((y + k) % 4) + core

    each(1, 4, lambda k: mx_out(k).start())
    pl.semaphore_wait(in_sem, 15)

    def mx_in(k):
        src = (y + 4 - k) % 4
        remote(m_cols.at[src], m_cols.at[src], mxs_sem.at[k], mxr_sem.at[src], i, sibling).wait_recv()

    each(1, 4, mx_in)
    total = jnp.zeros((72, 128), F32)
    for q in range(4):
        total = total + jnp.dot(m_cols[q], g_inv_ref[128 * q:128 * q + 128, here_y],
                                precision=lax.Precision.HIGHEST, preferred_element_type=F32)
    m_piece[...] = total
    m_to = 4 * a + i // 4

    def m_spot(rho, chunk):
        return m_rows.at[pl.ds(pl.multiple_of(72 * rho, 8), 72),
                         pl.ds(pl.multiple_of(128 * chunk, 128), 128)]

    m_here = 2 * (i % 4) + b % 2

    def mg_out(n):
        return remote(m_piece, m_spot(i % 4, b % 2), mgs_sem.at[n], mgr_sem.at[m_here], 8 * (b // 2) + n, m_to)

    def mg_mine(n):
        return (8 * (b // 2) + n == i) & (m_to == j)

    def mg_start(k):
        n = (z + k) % 8

        @pl.when(jnp.logical_not(mg_mine(n)))
        def _():
            mg_out(n).start()

        @pl.when(mg_mine(n))
        def _():
            pltpu.make_async_copy(m_piece, m_spot(i % 4, b % 2), mgr_sem.at[m_here]).start()

    each(0, 8, mg_start)

    def g_in(k):
        src = (j + 16 - k) % 16
        here = g_recv.at[src]
        remote(here, here, gs_sem.at[k], gr_sem.at[src], i, src).wait_recv()

    each(1, 16, g_in)
    total = g_recv[0].astype(F32)
    for k in range(1, 16):
        total = total + g_recv[k].astype(F32)
    g_sum[...] = total

    def g_spot(ref, who):
        return ref.at[pl.ds(pl.multiple_of(8 * (who // 4), 8), 8),
                      pl.ds(pl.multiple_of(128 * (who % 4), 128), 128)]

    def g2_out(k):
        to = (i + k) % 16
        return remote(g_spot(g_sum, to), g2_recv.at[i], g2s_sem.at[k], g2r_sem.at[i], to, j)

    each(1, 16, lambda k: g2_out(k).start())
    g2_recv[pl.ds(i, 1)] = g_sum[pl.ds(pl.multiple_of(8 * (i // 4), 8), 8),
                                 pl.ds(pl.multiple_of(128 * (i % 4), 128), 128)][None]

    @pl.when(i < 15)
    def _():
        def a_in(k):
            src = (i + 16 - k) % 16
            here = a_recv.at[src]
            remote(here, here, as_sem.at[0], ar_sem.at[src], src, j).wait_recv()

        each(1, 16, a_in)
        for half in range(2):
            span = slice(128 * half, 128 * half + 128)
            total = a_recv[0, span].astype(F32)
            for k in range(1, 16):
                total = total + a_recv[k, span].astype(F32)
            a_sum[2 * half] = total
            a_sum[2 * half + 1] = total.T

    def spread(act):
        def one(n):
            half = n // 32
            turned = (n // 16) % 2
            yp, xp, tj, ti = (n // 8) % 2, (n // 4) % 2, (n // 2) % 2, n % 2
            k = 2 * i + half
            flat = k < 15
            ey = jnp.where(flat, 0, jnp.where(k < 22, 1, 2))
            s = jnp.where(flat, k % 5, (k + 6) % 7)
            ex = jnp.where(s < 3, 0, jnp.where(s < 5, s - 2, 4 - s))
            row_y = jnp.where(flat, k // 5, yp)
            row_x = jnp.where(s < 3, s, jnp.where(s < 5, 0, s - 4)) + xp
            ok = (k < BLOCKS) & ((yp == 0) | (ey == 1)) & ((xp == 0) | (ex == 1) | (ex == -1))
            ok = ok & ((turned == 0) | (ey != 0) | (ex != 0))
            first = 4 * (3 * row_y + row_x) + a
            second = 4 * (3 * (row_y + ey) + row_x + ex) + b
            r = jnp.where(turned == 0, first, second)
            c = jnp.where(turned == 0, second, first)
            to_j = (4 * r) // 9 + tj
            to_i = (4 * c) // 9 + ti
            ok = ok & (to_j <= (128 * r + 127) // 288) & (to_i <= (128 * c + 127) // 288)
            at_r = r - (9 * to_j) // 4
            at_c = c - (9 * to_i) // 4
            src = a_sum.at[2 * half + turned]
            dst = tile.at[pl.ds(pl.multiple_of(128 * at_r, 128), 128),
                          pl.ds(pl.multiple_of(128 * at_c, 128), 128)]
            mine = (to_i == i) & (to_j == j)
            arrived = tr_sem.at[3 * at_r + at_c]

            @pl.when(ok & jnp.logical_not(mine))
            def _():
                act(remote(src, dst, ts_sem.at[n], arrived, to_i, to_j))

            if act is start:
                @pl.when(ok & mine)
                def _():
                    pltpu.make_async_copy(src, dst, arrived).start()

        each(0, 64, one)

    def start(copy):
        copy.start()

    def sent_off(copy):
        copy.wait_send()

    spread(start)

    for q in range(8):
        here = m_spot(q // 2, q % 2)
        remote(here, here, mgs_sem.at[0], mgr_sem.at[q], i, sibling).wait_recv()
    inv_out.wait_recv()
    lane = lax.broadcasted_iota(jnp.int32, (72, 128), 1) // 32
    for t in range(2):
        prod = jnp.dot(inv_both[t], m_rows[...], precision=lax.Precision.HIGHEST,
                       preferred_element_type=F32)
        for to in range(8):
            piece = jnp.zeros((72, 128), F32)
            for q in range(4):
                block = prod[72 * q:72 * q + 72, 128 * (to // 4):128 * (to // 4) + 128]
                shift = (32 * (q - to % 4)) % 128
                if shift:
                    block = pltpu.roll(block, shift, 1)
                piece = jnp.where(lane == q, block, piece)
            n_send[8 * t + to] = piece
    def n_out(n):
        return remote(n_send.at[n], n_recv.at[j], ns_sem.at[n], nr_sem.at[j], 8 * (n // 8) + z, 8 * xl + n % 8)

    def n_mine(n):
        return (n // 8 == xl) & (8 * xl + n % 8 == j)

    def n_start(k):
        n = (k + j) % 16

        @pl.when(jnp.logical_not(n_mine(n)))
        def _():
            n_out(n).start()

    each(0, 16, n_start)

    @pl.when(xl == j // 8)
    def _():
        n_recv[pl.ds(j, 1)] = n_send[pl.ds(j, 1)]

    def g2_in(k):
        src = (i + 16 - k) % 16
        here = g2_recv.at[src]
        remote(here, here, g2s_sem.at[k], g2r_sem.at[src], src, j).wait_recv()

    each(1, 16, g2_in)
    total = g2_recv[0]
    for k in range(1, 16):
        total = total + g2_recv[k]
    g_piece[...] = total

    def g3_out(k):
        return remote(g_piece, g_spot(g_fin, i), g3s_sem.at[k], g3r_sem.at[i], (i + k) % 16, j)

    each(1, 16, lambda k: g3_out(k).start())
    g_fin[pl.ds(pl.multiple_of(8 * (i // 4), 8), 8),
          pl.ds(pl.multiple_of(128 * (i % 4), 128), 128)] = total

    def c_in(k):
        q = (y + 4 - k) % 4
        here = c_recv.at[:, pl.ds(pl.multiple_of(128 * q, 128), 128)]
        remote(here, here, cs_sem.at[k], cr_sem.at[q], i, sibling).wait_recv()

    each(1, 4, c_in)
    conv_ref[...] = c_recv[...]

    for q in range(9):
        here = tile.at[pl.ds(128 * (q // 3), 128), pl.ds(128 * (q % 3), 128)]
        remote(here, here, ts_sem.at[0], tr_sem.at[q], i, sibling).wait_recv()
    rows = tile[pl.ds(pl.multiple_of(32 * (j % 4), 32), 288), :]
    rows = pltpu.roll(rows, (384 - 32 * (i % 4)) % 384, 1)[:, 0:288]
    a_ref[...] = 0.5 * a_old_ref[...] + (0.5 / 65536.0) * rows

    def g3_in(k):
        src = (i + 16 - k) % 16
        here = g_spot(g_fin, src)
        remote(here, here, g3s_sem.at[k], g3r_sem.at[src], src, j).wait_recv()

    each(1, 16, g3_in)
    g_ref[...] = 0.5 * g_old_ref[...] + 0.5 * g_fin[...]

    def n_in(src):
        @pl.when(jnp.logical_not((src == j) & (xl == j // 8)))
        def _():
            here = n_recv.at[src]
            remote(here, here, ns_sem.at[0], nr_sem.at[src], i, sibling).wait_recv()

    each(0, 16, n_in)
    total = n_recv[0]
    for k in range(1, 16):
        total = total + n_recv[k]
    ng_ref[...] = total

    for n in range(4):
        x_own(n).wait_send()
    for n in range(2):
        x_pass(n).wait_send()
        x_half(0, n).wait_send()
        x_half(1, n).wait_send()
    inv_out.wait_send()
    z_sib.wait_send()
    each(1, 8, lambda k: z_out(k).wait_send())

    def handed(k):
        who = (j + 2 * k) % 16
        x_fwd(who).wait_send()
        z_fwd(who).wait_send()

    each(1, 8, handed)
    w_each(lambda k: w_out(k).wait_send())
    w_each(lambda k: w_fwd(k).wait_send())
    each(1, 4, lambda k: mx_out(k).wait_send())
    each(1, 4, lambda k: c_out(k).wait_send())

    def rest_sent(k):
        g_out(k).wait_send()
        m_out(k).wait_send()
        g2_out(k).wait_send()
        g3_out(k).wait_send()

    each(1, 16, rest_sent)

    def a_sent(to):
        @pl.when(to != i)
        def _():
            a_out(to).wait_send()

    each(0, 15, a_sent)

    def mg_sent(n):
        @pl.when(jnp.logical_not(mg_mine(n)))
        def _():
            mg_out(n).wait_send()

    each(0, 8, mg_sent)

    def n_sent(n):
        @pl.when(jnp.logical_not(n_mine(n)))
        def _():
            n_out(n).wait_send()

    each(0, 16, n_sent)
    spread(sent_off)


def per_device(activations, cotangent, weight, a_factor_old, g_factor_old, a_inverse, g_inverse):
    vmem = pl.BlockSpec(memory_space=pltpu.VMEM)
    dma = pltpu.SemaphoreType.DMA
    conv, a_factor, g_factor, packed = pl.pallas_call(
        kernel,
        name="kfac_step",
        out_shape=(
            jax.ShapeDtypeStruct((256, 512), BF16),
            jax.ShapeDtypeStruct((288, 288), F32),
            jax.ShapeDtypeStruct((32, 512), F32),
            jax.ShapeDtypeStruct((72, 128), F32),
        ),
        in_specs=[vmem] * 7,
        out_specs=(vmem,) * 4,
        scratch_shapes=[
            pltpu.VMEM((16, 288, 512), BF16),
            pltpu.VMEM((512, 256), BF16),
            pltpu.VMEM((384, 256), BF16),
            pltpu.VMEM((288, 384), BF16),
            pltpu.VMEM((16, 256, 128), BF16),
            pltpu.VMEM((3, 288, 128), BF16),
            pltpu.VMEM((4608, 128), BF16),
            pltpu.VMEM((5, 384, 384), F32),
            pltpu.VMEM((2, 288, 288), F32),
            pltpu.VMEM((1152, 128), F32),
            pltpu.VMEM((16, 72, 128), F32),
            pltpu.VMEM((4, 72, 128), F32),
            pltpu.VMEM((72, 128), F32),
            pltpu.VMEM((288, 256), F32),
            pltpu.VMEM((16, 72, 128), F32),
            pltpu.VMEM((16, 72, 128), F32),
            pltpu.VMEM((3840, 128), BF16),
            pltpu.VMEM((16, 256, 128), BF16),
            pltpu.VMEM((4, 128, 128), F32),
            pltpu.VMEM((384, 384), F32),
            pltpu.VMEM((512, 512), BF16),
            pltpu.VMEM((16, 32, 512), BF16),
            pltpu.VMEM((32, 512), F32),
            pltpu.VMEM((16, 8, 128), F32),
            pltpu.VMEM((8, 128), F32),
            pltpu.VMEM((32, 512), F32),
            pltpu.VMEM((4, 256, 128), BF16),
            pltpu.VMEM((256, 512), BF16),
            pltpu.SemaphoreType.REGULAR,
            dma((2,)),
            dma((10,)), dma((16,)), dma((16,)), dma((16,)),
            dma((8,)), dma((16,)), dma((8,)),
            dma((16,)), dma((16,)), dma((16,)),
            dma((16,)), dma((16,)), dma((4,)), dma((4,)), dma((16,)), dma((16,)),
            dma((16,)), dma((16,)),
            dma((16,)), dma((16,)), dma((64,)), dma((9,)),
            dma((16,)), dma((16,)), dma((16,)), dma((16,)), dma((16,)), dma((16,)),
            dma((4,)), dma((4,)),
        ],
        compiler_params=pltpu.CompilerParams(
            collective_id=0, has_side_effects=True, vmem_limit_bytes=56 * 1024 * 1024),
        cost_estimate=pl.CostEstimate(flops=15_000_000_000, bytes_accessed=4_000_000, transcendentals=0),
    )(activations.reshape(256, 512), cotangent.reshape(256, 512), weight, a_factor_old, g_factor_old, a_inverse, g_inverse)
    natural = packed.reshape(72, 4, 32).transpose(1, 0, 2).reshape(288, 32).astype(BF16)
    return conv.reshape(1, 16, 16, 512), a_factor, g_factor, natural


def solution(mesh):
    return jax.shard_map(
        per_device,
        mesh=mesh,
        in_specs=(
            P(("fsdp", "factor"), None, None, None),
            P(("fsdp", "factor"), None, None, None),
            P("fsdp", None),
            P("factor", "fsdp"),
            P("factor", None),
            P("fsdp", "factor"),
            P(),
        ),
        out_specs=(
            P(("fsdp", "factor"), None, None, None),
            P("factor", "fsdp"),
            P("factor", None),
            P("fsdp", "factor"),
        ),
        check_vma=False,
    )
```

time: 166 us -> 140 us (0.84)
  Pallas kernels: 161 us -> 134 us
    pallas_call x1, Pallas kernels: 161 us -> 134 us  [per_device(): pl.pallas_call(kernel, name='kfac_step', out_shape=(jax.ShapeDtypeStruct(...]
where the time goes in v2:
time: 140 us; the launch traced here: 139 us
  Pallas kernels  134 us (96%)
  local copies, waits for them, and re-layouts  4.01 us (3%)
    pallas_call x1, Pallas kernels, per_device(): pl.pallas_call(kernel, name='kfac_step', out_shape=(jax.ShapeDtypeStruct(...  134 us
    unnamed x7, local copies, waits for them, and re-layouts  3.16 us

profile of v2, /device:TPU:184, one launch (start us, length us, event | category | flops | bytes accessed | tf_op | source)
XLA Modules:
  0.0 139.5 jit_solution(12447942888450982220)
XLA Ops:
  0.6 134.0 %kfac_step.1 = (bf16[256,512]{1,0:T(8,128)(2,1)}, f32[288,288]{1,0:T(8,128)}, f32[32,512]{1,0:T(8,128)}, f32[72,128]{1,0:T(8,128)}) custom-call(bf16[256,512]{1,0:T(8,128)(2,1)} %bitcast.10, bf16[256,512]{1,0:T(8,128)(2,1)} %bitcast.11, bf16[288,512]{1,0:T(8,128)(2,1)} %w_ref.1, f32[288,288]{1,0:T(8,128)} %a_old_ref.1, f32[32,512]{1,0:T(8,128)} %g_old_ref.1, ...), custom_call_target="tpu_custom_call" | custom-call | flops 15000000512 | bytes 4000000 | tf_op jit(solution)/shard_map/kfac_step/pallas_call | solution.py:615
  134.6 0.0 copy-start
  134.6 0.8 convert_element_type.12
  135.5 0.1 copy.13
  135.6 0.7 convert_element_type.15
  136.3 1.7 %copy.18 = bf16[1,16,16,512]{3,2,1,0:T(8,128)(2,1)} copy(bf16[1,16,16,512]{3,2,1,0:T(8,128)(2,1)} %bitcast.8) | data formatting | bytes 524288
  138.0 0.0 copy-done
  138.0 0.0 copy-start.1
  138.0 0.8 copy.19
  138.8 0.1 copy-done.1
  138.9 0.6 copy.20
  (1 shorter events, 0.0 us)
Async XLA Ops:
  134.6 3.4 %copy-start = (f32[288,288]{1,0:T(8,128)S(1)}, f32[288,288]{1,0:T(8,128)}, u32[]{:S(2)}) copy-start(f32[288,288]{1,0:T(8,128)} %get-tuple-element.17) | copy-start | bytes 995332
  138.0 0.9 copy-start.1

commit v3 on v2

--- a/solution.py
+++ b/solution.py
@@ -10,11 +10,15 @@
 BF16 = jnp.bfloat16
 X_BLOCKS = ((0, 0), (1, 1), (2, 2), (0, 1), (0, 2), (1, 0), (2, 0))
 COUNTS = (5, 5, 5, 7, 7)
-BLOCKS = 29
+SLOTS = (
+    1, 22, 15, 25, 4, 21, 20, 2, 23, 11, 28, 14, 5, 17, 8, 13,
+    19, 12, 3, 9, 10, 18, 16, 27, -1, -1, -1, 6, 26, 24, 0, 7,
+)
+IDLE = 12
 
 
 def kernel(
-    x_ref, dy_ref, w_ref, a_old_ref, g_old_ref, a_inv_ref, g_inv_ref,
+    x_ref, dy_ref, w_ref, a_inv_ref, g_inv_ref,
     conv_ref, a_ref, g_ref, ng_ref,
     x_all, x_t, xa_t, xb, z_all, z_sh, w_all, a_acc, inv_both,
     m_part, m_recv, m_cols, m_piece, m_rows, n_send, n_recv,
@@ -109,10 +113,7 @@
             return carry
         lax.fori_loop(0, 7 + core, step, 0)
 
-    w_each(lambda k: w_out(k).start())
-
     inv_out = remote(a_inv_ref, inv_both.at[xl], inv_sem.at[0], inv_sem.at[1], (i + 8) % 16, j)
-    inv_out.start()
 
     def clear(who):
         x_all[pl.ds(who, 1), 0:16] = jnp.zeros((1, 16, 512), BF16)
@@ -198,6 +199,7 @@
             x_pass(0).start()
             x_pass(1).start()
             hand_on(image(1, 0))
+            w_each(lambda k: w_out(k).start())
 
         @pl.when(n == 3)
         def _():
@@ -243,14 +245,13 @@
         w_in(k)
         w_fwd(k).start()
 
-    w_each(w_forward)
-
     def m_out(k):
         to = (i + k) % 16
         return remote(m_part.at[pl.ds(pl.multiple_of(72 * to, 8), 72)], m_recv.at[i],
                       ms_sem.at[k], mr_sem.at[i], to, j)
 
     each(1, 16, lambda k: m_out(k).start())
+    inv_out.start()
     m_recv[pl.ds(i, 1)] = m_part[pl.ds(pl.multiple_of(72 * i, 8), 72)][None]
 
     cot = dy_ref[...]
@@ -265,31 +266,40 @@
     each(1, 16, lambda k: g_out(k).start())
     g_recv[pl.ds(j, 1)] = g_send[pl.ds(pl.multiple_of(32 * j, 32), 32)][None]
 
-    def a_out(to):
-        return remote(a_send.at[pl.ds(pl.multiple_of(256 * to, 256), 256)], a_recv.at[i],
-                      as_sem.at[to], ar_sem.at[i], to, j)
-
-    def a_start(to):
-        @pl.when(to != i)
-        def _():
-            a_out(to).start()
-
-    at_block, sent = 0, 0
+    own_slot = (i + 11 * j) % 16
+
+    def a_to(slot):
+        return (slot + 5 * j) % 16
+
+    def a_out(slot):
+        return remote(a_send.at[pl.ds(pl.multiple_of(256 * slot, 256), 256)], a_recv.at[i],
+                      as_sem.at[slot], ar_sem.at[i], a_to(slot), j)
+
+    def a_start(k):
+        slot = (own_slot + k) % 16
+
+        @pl.when(slot != IDLE)
+        def _():
+            a_out(slot).start()
+
+    at_block = 0
     for combo, count in enumerate(COUNTS):
         part = a_acc[combo]
         for row_x, col_x in X_BLOCKS[:count]:
-            a_send[128 * at_block:128 * at_block + 128, :] = part[
+            spot = 128 * SLOTS.index(at_block)
+            a_send[spot:spot + 128, :] = part[
                 128 * row_x:128 * row_x + 128, 128 * col_x:128 * col_x + 128].astype(BF16)
             at_block += 1
-        if at_block == BLOCKS:
-            a_send[128 * BLOCKS:128 * BLOCKS + 128, :] = jnp.zeros((128, 128), BF16)
-            at_block += 1
-        each(sent, at_block // 2, a_start)
-        sent = at_block // 2
-
-    @pl.when(i < 15)
+    for spot, block in enumerate(SLOTS):
+        if block < 0:
+            a_send[128 * spot:128 * spot + 128, :] = jnp.zeros((128, 128), BF16)
+    each(1, 16, a_start)
+
+    @pl.when(own_slot != IDLE)
     def _():
-        a_recv[pl.ds(i, 1)] = a_send[pl.ds(pl.multiple_of(256 * i, 256), 256)][None]
+        a_recv[pl.ds(i, 1)] = a_send[pl.ds(pl.multiple_of(256 * own_slot, 256), 256)][None]
+
+    w_each(w_forward)
 
     def w_other(k):
         @pl.when(k % 2 != core)
@@ -404,7 +414,7 @@
     g2_recv[pl.ds(i, 1)] = g_sum[pl.ds(pl.multiple_of(8 * (i // 4), 8), 8),
                                  pl.ds(pl.multiple_of(128 * (i % 4), 128), 128)][None]
 
-    @pl.when(i < 15)
+    @pl.when(own_slot != IDLE)
     def _():
         def a_in(k):
             src = (i + 16 - k) % 16
@@ -420,45 +430,59 @@
             a_sum[2 * half] = total
             a_sum[2 * half + 1] = total.T
 
+    def block_in(slot):
+        block = jnp.int32(-1)
+        for spot, held in enumerate(SLOTS):
+            block = jnp.where(slot == spot, held, block)
+        return block
+
     def spread(act):
-        def one(n):
-            half = n // 32
-            turned = (n // 16) % 2
-            yp, xp, tj, ti = (n // 8) % 2, (n // 4) % 2, (n // 2) % 2, n % 2
-            k = 2 * i + half
+        for half in range(2):
+            k = block_in(2 * own_slot + half)
             flat = k < 15
             ey = jnp.where(flat, 0, jnp.where(k < 22, 1, 2))
-            s = jnp.where(flat, k % 5, (k + 6) % 7)
+            s = jnp.where(flat, (k + 5) % 5, (k + 6) % 7)
             ex = jnp.where(s < 3, 0, jnp.where(s < 5, s - 2, 4 - s))
-            row_y = jnp.where(flat, k // 5, yp)
-            row_x = jnp.where(s < 3, s, jnp.where(s < 5, 0, s - 4)) + xp
-            ok = (k < BLOCKS) & ((yp == 0) | (ey == 1)) & ((xp == 0) | (ex == 1) | (ex == -1))
-            ok = ok & ((turned == 0) | (ey != 0) | (ex != 0))
-            first = 4 * (3 * row_y + row_x) + a
-            second = 4 * (3 * (row_y + ey) + row_x + ex) + b
-            r = jnp.where(turned == 0, first, second)
-            c = jnp.where(turned == 0, second, first)
-            to_j = (4 * r) // 9 + tj
-            to_i = (4 * c) // 9 + ti
-            ok = ok & (to_j <= (128 * r + 127) // 288) & (to_i <= (128 * c + 127) // 288)
-            at_r = r - (9 * to_j) // 4
-            at_c = c - (9 * to_i) // 4
-            src = a_sum.at[2 * half + turned]
-            dst = tile.at[pl.ds(pl.multiple_of(128 * at_r, 128), 128),
-                          pl.ds(pl.multiple_of(128 * at_c, 128), 128)]
-            mine = (to_i == i) & (to_j == j)
-            arrived = tr_sem.at[3 * at_r + at_c]
-
-            @pl.when(ok & jnp.logical_not(mine))
-            def _():
-                act(remote(src, dst, ts_sem.at[n], arrived, to_i, to_j))
-
-            if act is start:
-                @pl.when(ok & mine)
+            low_x = jnp.where(s < 3, s, jnp.where(s < 5, 0, s - 4))
+            low_y = jnp.where(flat, (k + 5) // 5 - 1, 0)
+
+            def place(n):
+                turned, yp, xp = n // 4, (n // 2) % 2, n % 2
+                ok = (k >= 0) & ((yp == 0) | (ey == 1)) & ((xp == 0) | (ex == 1) | (ex == -1))
+                ok = ok & ((turned == 0) | (ey != 0) | (ex != 0))
+
+                @pl.when(ok)
                 def _():
-                    pltpu.make_async_copy(src, dst, arrived).start()
-
-        each(0, 64, one)
+                    row_y, row_x = low_y + yp, low_x + xp
+                    first = 4 * (3 * row_y + row_x) + a
+                    second = 4 * (3 * (row_y + ey) + row_x + ex) + b
+                    r = jnp.where(turned == 0, first, second)
+                    c = jnp.where(turned == 0, second, first)
+                    src = a_sum.at[2 * half + turned]
+                    for t in range(4):
+                        to_j = (4 * r) // 9 + t // 2
+                        to_i = (4 * c) // 9 + t % 2
+                        inside = (to_j <= (128 * r + 127) // 288) & (to_i <= (128 * c + 127) // 288)
+                        at_r = r - (9 * to_j) // 4
+                        at_c = c - (9 * to_i) // 4
+                        mine = (to_i == i) & (to_j == j)
+
+                        @pl.when(inside)
+                        def _():
+                            dst = tile.at[pl.ds(pl.multiple_of(128 * at_r, 128), 128),
+                                          pl.ds(pl.multiple_of(128 * at_c, 128), 128)]
+                            arrived = tr_sem.at[3 * at_r + at_c]
+
+                            @pl.when(jnp.logical_not(mine))
+                            def _():
+                                act(remote(src, dst, ts_sem.at[32 * half + 4 * n + t], arrived, to_i, to_j))
+
+                            if act is start:
+                                @pl.when(mine)
+                                def _():
+                                    pltpu.make_async_copy(src, dst, arrived).start()
+
+            each(0, 8, place)
 
     def start(copy):
         copy.start()
@@ -535,7 +559,7 @@
         remote(here, here, ts_sem.at[0], tr_sem.at[q], i, sibling).wait_recv()
     rows = tile[pl.ds(pl.multiple_of(32 * (j % 4), 32), 288), :]
     rows = pltpu.roll(rows, (384 - 32 * (i % 4)) % 384, 1)[:, 0:288]
-    a_ref[...] = 0.5 * a_old_ref[...] + (0.5 / 65536.0) * rows
+    a_ref[...] = rows
 
     def g3_in(k):
         src = (i + 16 - k) % 16
@@ -543,7 +567,7 @@
         remote(here, here, g3s_sem.at[k], g3r_sem.at[src], src, j).wait_recv()
 
     each(1, 16, g3_in)
-    g_ref[...] = 0.5 * g_old_ref[...] + 0.5 * g_fin[...]
+    g_ref[...] = g_fin[...]
 
     def n_in(src):
         @pl.when(jnp.logical_not((src == j) & (xl == j // 8)))
@@ -586,12 +610,12 @@
 
     each(1, 16, rest_sent)
 
-    def a_sent(to):
-        @pl.when(to != i)
-        def _():
-            a_out(to).wait_send()
-
-    each(0, 15, a_sent)
+    def a_sent(slot):
+        @pl.when((slot != IDLE) & (slot != own_slot))
+        def _():
+            a_out(slot).wait_send()
+
+    each(0, 16, a_sent)
 
     def mg_sent(n):
         @pl.when(jnp.logical_not(mg_mine(n)))
@@ -607,6 +631,15 @@
 
     each(0, 16, n_sent)
     spread(sent_off)
+
+
+def finish(conv_ref, a_sum_ref, g_sum_ref, packed_ref, a_old_ref, g_old_ref, out_ref, a_ref, g_ref, ng_ref):
+    out_ref[...] = conv_ref[...]
+    a_ref[...] = 0.5 * a_old_ref[...] + (0.5 / 65536.0) * a_sum_ref[...]
+    g_ref[...] = 0.5 * g_old_ref[...] + 0.5 * g_sum_ref[...]
+    packed = packed_ref[...]
+    rows = [packed[:, 0:32]] + [pltpu.roll(packed, 128 - 32 * q, 1)[:, 0:32] for q in range(1, 4)]
+    ng_ref[...] = jnp.concatenate(rows, axis=0).T.astype(BF16)
 
 
 def per_device(activations, cotangent, weight, a_factor_old, g_factor_old, a_inverse, g_inverse):
@@ -621,7 +654,7 @@
             jax.ShapeDtypeStruct((32, 512), F32),
             jax.ShapeDtypeStruct((72, 128), F32),
         ),
-        in_specs=[vmem] * 7,
+        in_specs=[vmem] * 5,
         out_specs=(vmem,) * 4,
         scratch_shapes=[
             pltpu.VMEM((16, 288, 512), BF16),
@@ -640,7 +673,7 @@
             pltpu.VMEM((288, 256), F32),
             pltpu.VMEM((16, 72, 128), F32),
             pltpu.VMEM((16, 72, 128), F32),
-            pltpu.VMEM((3840, 128), BF16),
+            pltpu.VMEM((4096, 128), BF16),
             pltpu.VMEM((16, 256, 128), BF16),
             pltpu.VMEM((4, 128, 128), F32),
             pltpu.VMEM((384, 384), F32),
@@ -666,9 +699,21 @@
         compiler_params=pltpu.CompilerParams(
             collective_id=0, has_side_effects=True, vmem_limit_bytes=56 * 1024 * 1024),
         cost_estimate=pl.CostEstimate(flops=15_000_000_000, bytes_accessed=4_000_000, transcendentals=0),
-    )(activations.reshape(256, 512), cotangent.reshape(256, 512), weight, a_factor_old, g_factor_old, a_inverse, g_inverse)
-    natural = packed.reshape(72, 4, 32).transpose(1, 0, 2).reshape(288, 32).astype(BF16)
-    return conv.reshape(1, 16, 16, 512), a_factor, g_factor, natural
+    )(activations.reshape(256, 512), cotangent.reshape(256, 512), weight, a_inverse, g_inverse)
+    conv, a_factor, g_factor, natural = pl.pallas_call(
+        finish,
+        name="finish",
+        out_shape=(
+            jax.ShapeDtypeStruct((256, 512), BF16),
+            jax.ShapeDtypeStruct((288, 288), F32),
+            jax.ShapeDtypeStruct((32, 512), F32),
+            jax.ShapeDtypeStruct((32, 288), BF16),
+        ),
+        in_specs=[vmem] * 6,
+        out_specs=(vmem,) * 4,
+        cost_estimate=pl.CostEstimate(flops=1_000_000, bytes_accessed=2_000_000, transcendentals=0),
+    )(conv, a_factor, g_factor, packed, a_factor_old, g_factor_old)
+    return conv.reshape(1, 16, 16, 512), a_factor, g_factor, natural.T
 
 
 def solution(mesh):

time: 140 us -> 120 us (0.86)
  the two profiles are of different devices: /device:TPU:184 before, /device:TPU:37 now
where the time goes in v3:
time: 120 us; the launch traced here: 119 us
  Pallas kernels  119 us (99%)
    pallas_call x1, Pallas kernels, per_device(): pl.pallas_call(kernel, name='kfac_step', out_shape=(jax.ShapeDtypeStruct(...  116 us

profile of v3, /device:TPU:37, one launch (start us, length us, event | category | flops | bytes accessed | tf_op | source)
XLA Modules:
  0.0 119.4 jit_solution(5178801446558416049)
XLA Ops:
  0.6 116.4 %kfac_step.1 = (bf16[256,512]{1,0:T(8,128)(2,1)}, f32[288,288]{1,0:T(8,128)}, f32[32,512]{1,0:T(8,128)}, f32[72,128]{1,0:T(8,128)}) custom-call(bf16[256,512]{1,0:T(8,128)(2,1)} %bitcast.4, bf16[256,512]{1,0:T(8,128)(2,1)} %bitcast.5, bf16[288,512]{1,0:T(8,128)(2,1)} %w_ref.1, f32[288,288]{1,0:T(8,128)} %a_inv_ref.1, f32[512,512]{1,0:T(8,128)} %g_inv_ref.1), custom_call_target="tpu_custom_call" | custom-call | flops 15000000512 | bytes 4000000 | tf_op jit(solution)/shard_map/kfac_step/pallas_call | solution.py:648
  117.1 2.3 %finish.1 = (bf16[256,512]{1,0:T(8,128)(2,1)}, f32[288,288]{1,0:T(8,128)}, f32[32,512]{1,0:T(8,128)}, bf16[32,288]{1,0:T(8,128)(2,1)}) custom-call(bf16[256,512]{1,0:T(8,128)(2,1)} %get-tuple-element.12.conv_ref, f32[288,288]{1,0:T(8,128)} %get-tuple-element.13.a_sum_ref, f32[32,512]{1,0:T(8,128)} %get-tuple-element.14.g_sum_ref, ...), custom_call_target="tpu_custom_call" | custom-call | flops 1000000 | bytes 2000000 | tf_op jit(solution)/shard_map/finish/pallas_call | solution.py:703

commit v4 on v3

--- a/solution.py
+++ b/solution.py
@@ -245,8 +245,14 @@
         w_in(k)
         w_fwd(k).start()
 
+    def far_first(k):
+        n = k - 1 + k // 15
+        t = n // 2
+        dz = jnp.where(t % 2 == 0, 4 + t // 2, 4 - (t + 1) // 2)
+        return 8 * ((xl + n % 2) % 2) + (z + dz) % 8
+
     def m_out(k):
-        to = (i + k) % 16
+        to = far_first(k)
         return remote(m_part.at[pl.ds(pl.multiple_of(72 * to, 8), 72)], m_recv.at[i],
                       ms_sem.at[k], mr_sem.at[i], to, j)
 
@@ -276,7 +282,7 @@
                       as_sem.at[slot], ar_sem.at[i], a_to(slot), j)
 
     def a_start(k):
-        slot = (own_slot + k) % 16
+        slot = (far_first(k) + 11 * j) % 16
 
         @pl.when(slot != IDLE)
         def _():
@@ -293,7 +299,6 @@
     for spot, block in enumerate(SLOTS):
         if block < 0:
             a_send[128 * spot:128 * spot + 128, :] = jnp.zeros((128, 128), BF16)
-    each(1, 16, a_start)
 
     @pl.when(own_slot != IDLE)
     def _():
@@ -333,6 +338,8 @@
 
     each(1, 4, lambda k: c_out(k).start())
     c_recv[:, here_y] = c_send[y]
+
+    each(1, 16, a_start)
 
     def m_in(k):
         src = (i + 16 - k) % 16

time: 120 us -> 118 us (0.983)
  the two profiles are of different devices: /device:TPU:37 before, /device:TPU:45 now
where the time goes in v4:
time: 118 us
  Pallas kernels  117 us (99%)
    pallas_call x1, Pallas kernels, per_device(): pl.pallas_call(kernel, name='kfac_step', out_shape=(jax.ShapeDtypeStruct(...  115 us

profile of v4, /device:TPU:45, one launch (start us, length us, event | category | flops | bytes accessed | tf_op | source)
XLA Modules:
  0.0 117.8 jit_solution(18061509604850861341)
XLA Ops:
  0.6 114.8 %kfac_step.1 = (bf16[256,512]{1,0:T(8,128)(2,1)}, f32[288,288]{1,0:T(8,128)}, f32[32,512]{1,0:T(8,128)}, f32[72,128]{1,0:T(8,128)}) custom-call(bf16[256,512]{1,0:T(8,128)(2,1)} %bitcast.4, bf16[256,512]{1,0:T(8,128)(2,1)} %bitcast.5, bf16[288,512]{1,0:T(8,128)(2,1)} %w_ref.1, f32[288,288]{1,0:T(8,128)} %a_inv_ref.1, f32[512,512]{1,0:T(8,128)} %g_inv_ref.1), custom_call_target="tpu_custom_call" | custom-call | flops 15000000512 | bytes 4000000 | tf_op jit(solution)/shard_map/kfac_step/pallas_call | solution.py:655
  115.5 2.3 %finish.1 = (bf16[256,512]{1,0:T(8,128)(2,1)}, f32[288,288]{1,0:T(8,128)}, f32[32,512]{1,0:T(8,128)}, bf16[32,288]{1,0:T(8,128)(2,1)}) custom-call(bf16[256,512]{1,0:T(8,128)(2,1)} %get-tuple-element.12.conv_ref, f32[288,288]{1,0:T(8,128)} %get-tuple-element.13.a_sum_ref, f32[32,512]{1,0:T(8,128)} %get-tuple-element.14.g_sum_ref, ...), custom_call_target="tpu_custom_call" | custom-call | flops 1000000 | bytes 2000000 | tf_op jit(solution)/shard_map/finish/pallas_call | solution.py:710
